TPU v7x, 512 devices: a whole 4x4x16 slice. The times are simulated.
512 devices in a mesh: dx: 16 (over z), dy: 4 (over y), band: 8 (over x, core).
Axes of the slice: x: 4, y: 4, z: 16, core: 2. Of those that a mesh axis runs over, the one named last changes fastest.
Arguments:
- vectors: bfloat16 [13, 512, 8192], P(None, 'band', ('dx', 'dy')), may hold values from -6 to 6
- inner_pairs: int32 [6, 8192], P(None, ('dx', 'dy')), may hold values from 0 to 127
- inner_count: int32 [8192], P(('dx', 'dy')), may hold values from 1 to 6, as said below
- inner_blocks: bfloat16 [6, 13, 13, 8192], P(None, None, None, ('dx', 'dy'))
- cross_x_blocks: bfloat16 [4, 13, 13, 1024], P(None, None, None, ('dx', 'dy'))
- cross_y_blocks: bfloat16 [4, 13, 13, 1024], P(None, None, None, ('dx', 'dy'))
- spectrum_top: float32 [1], replicated, may hold values from 8 to 12
- filter_cut: float32 [1], replicated, may hold values from -2 to -0.5
Outputs:
- filtered: bfloat16 [13, 512, 8192], P(None, 'band', ('dx', 'dy'))
- correlation: float32 [512, 512], P('band', ('dx', 'dy'))
- projected: float32 [512, 512], P('band', ('dx', 'dy'))
Inputs may be any that keep to these rules, and one draw needn't show every extreme that they name: `inner_count`: slots from an atom's count on are padding; some atom has all 6 slots live.
All inputs are finite; a program needn't handle non-finite values.
Results may differ from a plain program's by a relative error of at most 0.0083.
Values may be sent and summed in bfloat16 or wider, within the bound.
A program may use at most 64 MiB of HBM per device.

v0:
```python
import jax
import jax.numpy as jnp
from jax import lax
from jax.sharding import PartitionSpec as P


def shifted(value, axis, steps):
    count = lax.axis_size(axis)
    pairs = [(source, (source + steps) % count) for source in range(count)]
    return lax.ppermute(value, axis, pairs)


def padded(block, sides, width):
    for axis, dim in sides:
        count = lax.axis_size(axis)
        forward = [(i, i + 1) for i in range(count - 1)]
        forward.append((count - 1, 0))
        backward = [(target, source) for source, target in forward]
        low = lax.ppermute(
            lax.slice_in_dim(block, block.shape[dim] - width, None, axis=dim), axis, forward
        )
        high = lax.ppermute(lax.slice_in_dim(block, 0, width, axis=dim), axis, backward)
        block = jnp.concatenate([low, block, high], axis=dim)
    return block


def on_device(
    vectors,
    inner_pairs,
    inner_count,
    inner_blocks,
    cross_x_blocks,
    cross_y_blocks,
    spectrum_top,
    filter_cut,
):
    orbitals, vec_width, atom_count = vectors.shape
    slot_count = inner_pairs.shape[0]
    reach_count = cross_x_blocks.shape[0]
    group_size = atom_count // 16
    edge_size = 2 * group_size
    rim_start = atom_count - 8 * group_size
    west_blocks = shifted(cross_x_blocks, "dx", 1)
    south_blocks = shifted(cross_y_blocks, "dy", 1)
    live_mask = (jnp.arange(slot_count)[:, None] < inner_count[None, :]).astype(jnp.bfloat16)
    inner_live = inner_blocks * live_mask[:, None, None, :]
    choose_hit = jnp.arange(atom_count, dtype=jnp.int32)[:, None, None] == inner_pairs[None, :, :]
    choose_half = choose_hit.astype(jnp.bfloat16)
    choose_full = choose_hit.astype(jnp.float32)
    top_value = spectrum_top[0]
    cut_value = filter_cut[0]
    half_span = (top_value - cut_value) * 0.5
    centre = (top_value + cut_value) * 0.5

    def unpack(layer, member):
        pieces = layer.reshape(2, orbitals, vec_width, 2, group_size)[:, :, :, member]
        return pieces.transpose(1, 2, 0, 3).reshape(orbitals, vec_width, edge_size)

    def rolled(source):
        return jnp.stack([jnp.roll(source, -offset, axis=2) for offset in range(reach_count)])

    def shifted_sum(terms):
        summed = terms[0]
        for offset in range(1, reach_count):
            summed = summed + jnp.roll(terms[offset], offset, axis=2)
        return summed

    def interior(source):
        gathered = jnp.einsum(
            "ova,akb->pvkb".replace("p", "o"),
            source,
            choose_half,
            preferred_element_type=jnp.float32,
        ).astype(jnp.bfloat16)
        summed = jnp.einsum(
            "kopb,pvkb->ovb", inner_live, gathered, preferred_element_type=jnp.float32
        )
        back_terms = jnp.einsum(
            "kopb,ovb->pvkb", inner_live, source, preferred_element_type=jnp.float32
        )
        return summed + jnp.einsum(
            "pvkb,akb->pva", back_terms, choose_full, precision=lax.Precision.HIGHEST
        )

    def apply_ham(source):
        strips = source[:, :, rim_start:].reshape(orbitals, vec_width, 4, 2, group_size)
        x_part = strips[:, :, 0:2]
        y_part = strips[:, :, 2:4].transpose(0, 1, 3, 2, 4)
        tiles = jnp.concatenate([x_part, y_part], axis=4)
        tiles = tiles.transpose(2, 3, 0, 1, 4).reshape(2, 2, orbitals * vec_width * edge_size)
        extended = padded(tiles, (("dx", 0), ("dy", 1)), 1)
        from_west = unpack(extended[0, 1:3], 0)
        from_east = unpack(extended[3, 1:3], 0)
        from_south = unpack(extended[1:3, 0], 1)
        from_north = unpack(extended[1:3, 3], 1)
        east_forward = jnp.einsum(
            "mopt,mpvt->ovt", cross_x_blocks, rolled(from_east), preferred_element_type=jnp.float32
        )
        west_back = shifted_sum(
            jnp.einsum("mopt,ovt->mpvt", west_blocks, from_west, preferred_element_type=jnp.float32)
        )
        north_forward = jnp.einsum(
            "mopt,mpvt->ovt", cross_y_blocks, rolled(from_north), preferred_element_type=jnp.float32
        )
        south_back = shifted_sum(
            jnp.einsum(
                "mopt,ovt->mpvt", south_blocks, from_south, preferred_element_type=jnp.float32
            )
        )
        rim_sum = jnp.concatenate([west_back, east_forward, south_back, north_forward], axis=2)
        summed = interior(source)
        return summed.at[:, :, rim_start:].add(rim_sum)

    start_f = vectors.astype(jnp.float32)
    first_step = ((apply_ham(vectors) - centre * start_f) / half_span).astype(jnp.bfloat16)
    second_step = (
        2.0 * (apply_ham(first_step) - centre * first_step.astype(jnp.float32)) / half_span
        - start_f
    ).astype(jnp.bfloat16)
    filtered = (
        2.0 * (apply_ham(second_step) - centre * second_step.astype(jnp.float32)) / half_span
        - first_step.astype(jnp.float32)
    ).astype(jnp.bfloat16)
    image_next = ((apply_ham(filtered) - centre * filtered.astype(jnp.float32)) / half_span).astype(
        jnp.bfloat16
    )
    block_piece = lax.all_gather(filtered, "band", axis=1, tiled=True)
    correlation_part = jnp.einsum(
        "ova,owa->vw", filtered, block_piece, preferred_element_type=jnp.float32
    )
    projected_part = jnp.einsum(
        "ova,owa->vw", image_next, block_piece, preferred_element_type=jnp.float32
    )
    partials = jnp.stack([correlation_part, projected_part])
    summed_all = lax.psum_scatter(partials, ("dx", "dy"), scatter_dimension=2, tiled=True)
    normalize = 1.0 / float(orbitals * atom_count * lax.axis_size(("dx", "dy")))
    return (filtered, summed_all[0] * normalize, summed_all[1] * normalize)


def solution(mesh):
    in_specs = (
        P(None, "band", ("dx", "dy")),
        P(None, ("dx", "dy")),
        P(("dx", "dy")),
        P(None, None, None, ("dx", "dy")),
        P(None, None, None, ("dx", "dy")),
        P(None, None, None, ("dx", "dy")),
        P(),
        P(),
    )
    out_specs = (P(None, "band", ("dx", "dy")), P("band", ("dx", "dy")), P("band", ("dx", "dy")))
    return jax.shard_map(
        on_device, mesh=mesh, in_specs=in_specs, out_specs=out_specs, check_vma=False
    )
```

profile of v0, /device:TPU:6, one launch (start us, length us, event | category | flops | bytes accessed | tf_op | source)
XLA Modules:
  0.0 689.3 jit_solution(18433148698720118778)
XLA Ops:
  10.0 3.8 collective-permute-start
  14.6 9.5 %collective-permute-start.2 = (bf16[1,2,13312]{2,1,0:T(2,128)(2,1)S(1)}, bf16[1,2,13312]{2,1,0:T(2,128)(2,1)S(1)}, u32[]{:S(2)}, u32[]{:S(2)}) collective-permute-start(bf16[1,2,13312]{2,1,0:T(2,128)(2,1)S(1)} %slice.696), channel_id=1, source_target_pairs={{32,0},{64,32},{96,64},{128,96},{160,128},{192,160},{224,192},{256... | collective-permute-start | bytes 159752 | tf_op jit(solution)/shard_map/ppermute | solution.py:22
  25.4 3.5 collective-permute-start.4
  33.0 5.7 copy.269
  38.7 6.2 copy.268
  51.6 6.8 fusion.13
  60.9 6.5 copy.267
  67.4 5.1 fusion.9
  78.1 2.7 reshape.241
  86.9 2.7 reshape_squeeze.48
  89.6 3.4 copy.437
  97.3 3.6 collective-permute-start.5
  106.2 4.0 collective-permute-done.3
  113.1 3.3 slice.910
  120.6 2.7 reshape_squeeze.50
  123.3 3.3 slice.897
  126.7 3.4 copy.440
  134.7 3.6 convolution_bitcast_fusion.2
  148.9 5.1 collective-permute-start.7
  154.0 9.6 %fusion.16 = f32[13,64,128]{2,1,0:T(8,128)} fusion(f32[13,64,6,128]{1,0,2,3:T(8,128)} %convolution_bitcast_fusion.2, s32[6,128]{1,0:T(8,128)S(1)} %copy-done.24), kind=kOutput, calls=%fused_computation.38 | convolution fusion | flops 981565440 | bytes 2984960 | tf_op jit(solution)/shard_map/pvkb,akb->pva/dot_general | solution.py:81
  166.0 2.6 convolution_convert_fusion.2
  168.6 6.1 copy.300
  174.7 5.1 fusion.10
  182.0 2.7 reshape.247
  184.7 2.7 reshape_squeeze.52
  193.7 2.7 reshape_squeeze.53
  204.4 5.1 collective-permute-start.9
  215.5 3.3 slice.943
  227.5 3.3 slice.956
  239.3 3.6 convolution_bitcast_fusion.1
  253.3 5.1 collective-permute-start.11
  258.4 9.6 %fusion.19 = f32[13,64,128]{2,1,0:T(8,128)} fusion(f32[13,64,6,128]{1,0,2,3:T(8,128)} %convolution_bitcast_fusion.1, s32[6,128]{1,0:T(8,128)S(1)} %copy-done.24), kind=kOutput, calls=%fused_computation.39 | convolution fusion | flops 981565440 | bytes 2984960 | tf_op jit(solution)/shard_map/pvkb,akb->pva/dot_general | solution.py:81
  273.0 6.5 copy.329
  279.5 5.1 fusion.11
  286.8 2.7 reshape.253
  289.5 2.7 reshape_squeeze.56
  298.5 2.7 reshape_squeeze.57
  309.2 5.1 collective-permute-start.13
  320.3 3.3 slice.989
  331.7 3.3 slice.1002
  346.2 4.7 convolution_bitcast_fusion
  355.8 5.3 collective-permute-start.15
  361.1 8.9 %fusion.22 = f32[13,64,128]{2,1,0:T(8,128)S(1)} fusion(f32[13,64,6,128]{1,0,2,3:T(8,128)} %convolution_bitcast_fusion, s32[6,128]{1,0:T(8,128)S(1)} %copy-done.24), kind=kOutput, calls=%fused_computation.40 | convolution fusion | flops 981565440 | bytes 2984960 | tf_op jit(solution)/shard_map/pvkb,akb->pva/dot_general | solution.py:81
  371.4 2.8 convolution_convert_fusion
  374.2 6.4 copy.360
  380.6 4.2 fusion.12
  394.2 5.1 collective-permute-start.17
  421.3 259.4 %all-reduce.3.cloned.1.call-done = f32[2,64,512]{1,0,2:T(2,128)} async-done(((f32[2,64,512]{1,0,2:T(2,128)}), f32[2,64,512]{1,0,2:T(2,128)}) %all-reduce.3.cloned.1.call-update) | async-done | bytes 262160
  (369 shorter events, 196.2 us)
Async XLA Ops:
  7.2 16.9 %copy-start.29 = (bf16[4,13,13,16]{3,0,2,1:T(4,128)(2,1)S(1)}, bf16[4,13,13,16]{3,0,2,1:T(4,128)(2,1)}, u32[]{:S(2)}) copy-start(bf16[4,13,13,16]{3,0,2,1:T(4,128)(2,1)} %param.21) | copy-start | bytes 64900
  7.2 21.7 %copy-start.30 = (bf16[4,13,13,16]{3,0,2,1:T(4,128)(2,1)S(1)}, bf16[4,13,13,16]{3,0,2,1:T(4,128)(2,1)}, u32[]{:S(2)}) copy-start(bf16[4,13,13,16]{3,0,2,1:T(4,128)(2,1)} %param.20) | copy-start | bytes 64900
  7.2 25.0 %copy-start.32 = (s32[128]{0:T(128)S(1)}, s32[128]{0:T(128)}, u32[]{:S(2)}) copy-start(s32[128]{0:T(128)} %param.18) | copy-start | bytes 1540
  7.2 25.1 %copy-start.23 = (bf16[6,13,13,128]{3,2,1,0:T(8,128)(2,1)S(1)}, bf16[6,13,13,128]{3,2,1,0:T(8,128)(2,1)}, u32[]{:S(2)}) copy-start(bf16[6,13,13,128]{3,2,1,0:T(8,128)(2,1)} %param.19) | copy-start | bytes 778756
  7.2 406.9 %all-gather.2.cloned.1.call-start = ((), (), s32[]{:S(2)}) async-start(), calls=%async_computation | async-start | bytes 1916928 | tf_op jit(solution)/shard_map/all_gather | solution.py:127
  8.7 23.6 %copy-start.17 = (bf16[2,2,13,64,16]{3,4,0,1,2:T(8,128)(2,1)}, bf16[2,2,13,64,16]{3,4,0,1,2:T(8,128)(2,1)S(1)}, u32[]{:S(2)}) copy-start(bf16[2,2,13,64,16]{3,4,0,1,2:T(8,128)(2,1)S(1)} %maximum_bitcast_fusion) | copy-start | bytes 319492
  10.0 76.9 %collective-permute-start = (bf16[1,2,13312]{2,1,0:T(2,128)(2,1)}, bf16[1,2,13312]{2,1,0:T(2,128)(2,1)}, u32[]{:S(2)}, u32[]{:S(2)}) collective-permute-start(bf16[1,2,13312]{2,1,0:T(2,128)(2,1)} %slice.683), channel_id=1, source_target_pairs={{0,32},{32,64},{64,96},{96,128},{128,160},{160,192},{192,224},{224... | collective-permute-start | bytes 159752 | tf_op jit(solution)/shard_map/ppermute | solution.py:19
  14.6 66.2 %collective-permute-start.2 = (bf16[1,2,13312]{2,1,0:T(2,128)(2,1)S(1)}, bf16[1,2,13312]{2,1,0:T(2,128)(2,1)S(1)}, u32[]{:S(2)}, u32[]{:S(2)}) collective-permute-start(bf16[1,2,13312]{2,1,0:T(2,128)(2,1)S(1)} %slice.696), channel_id=1, source_target_pairs={{32,0},{64,32},{96,64},{128,96},{160,128},{192,160},{224,192},{256... | collective-permute-start | bytes 159752 | tf_op jit(solution)/shard_map/ppermute | solution.py:22
  25.4 104.7 %collective-permute-start.4 = (bf16[4,13,13,16]{1,2,0,3:T(8,128)(2,1)}, bf16[4,13,13,16]{1,2,0,3:T(8,128)(2,1)S(1)}, u32[]{:S(2)}, u32[]{:S(2)}) collective-permute-start(bf16[4,13,13,16]{1,2,0,3:T(8,128)(2,1)} %copy.290), channel_id=1, source_target_pairs={{0,8},{8,16},{16,24},{24,0},{1,9},{9,17},{17,25},{25,1},{2,10},{10... | collective-permute-start | bytes 64904 | tf_op jit(solution)/shard_map/ppermute | solution.py:10
  30.1 62.9 %collective-permute-start.1 = (bf16[4,13,13,16]{1,2,0,3:T(8,128)(2,1)}, bf16[4,13,13,16]{1,2,0,3:T(8,128)(2,1)}, u32[]{:S(2)}, u32[]{:S(2)}) collective-permute-start(bf16[4,13,13,16]{1,2,0,3:T(8,128)(2,1)} %copy.278), channel_id=1, source_target_pairs={{0,32},{32,64},{64,96},{96,128},{128,160},{160,192},{192,224},{224... | collective-permute-start | bytes 64904 | tf_op jit(solution)/shard_map/ppermute | solution.py:10
  33.0 14.1 %copy-start.24 = (s32[6,128]{1,0:T(8,128)S(1)}, s32[6,128]{1,0:T(8,128)}, u32[]{:S(2)}) copy-start(s32[6,128]{1,0:T(8,128)} %param.17) | copy-start | bytes 9220
  80.7 1.9 copy-start.27
  93.0 10.2 %copy-start.28 = (bf16[13,64,13]{1,0,2:T(8,128)(2,1)S(1)}, bf16[13,64,13]{1,0,2:T(8,128)(2,1)}, u32[]{:S(2)}) copy-start(bf16[13,64,13]{1,0,2:T(8,128)(2,1)} %slice.893) | copy-start | bytes 64900
  93.0 10.2 %copy-start.25 = (bf16[13,64,15]{1,0,2:T(8,128)(2,1)S(1)}, bf16[13,64,15]{1,0,2:T(8,128)(2,1)}, u32[]{:S(2)}) copy-start(bf16[13,64,15]{1,0,2:T(8,128)(2,1)} %slice.889) | copy-start | bytes 74884
  93.0 10.3 %copy-start.26 = (bf16[13,64,14]{1,0,2:T(8,128)(2,1)S(1)}, bf16[13,64,14]{1,0,2:T(8,128)(2,1)}, u32[]{:S(2)}) copy-start(bf16[13,64,14]{1,0,2:T(8,128)(2,1)} %slice.891) | copy-start | bytes 69892
  97.3 8.5 %collective-permute-start.5 = (bf16[4,1,13312]{2,1,0:T(2,128)(2,1)S(1)}, bf16[4,1,13312]{2,1,0:T(2,128)(2,1)S(1)}, u32[]{:S(2)}, u32[]{:S(2)}) collective-permute-start(bf16[4,1,13312]{2,1,0:T(2,128)(2,1)S(1)} %get-tuple-element.108), channel_id=1, source_target_pairs={{8,0},{16,8},{24,16},{0,24},{9,1},{17,9},{25,17},{1,25},{10,2},{18... | collective-permute-start | bytes 319496 | tf_op jit(solution)/shard_map/ppermute | solution.py:22
  100.9 9.3 %collective-permute-start.3 = (bf16[4,1,13312]{2,1,0:T(2,128)(2,1)S(1)}, bf16[4,1,13312]{2,1,0:T(2,128)(2,1)S(1)}, u32[]{:S(2)}, u32[]{:S(2)}) collective-permute-start(bf16[4,1,13312]{2,1,0:T(2,128)(2,1)S(1)} %get-tuple-element.107), channel_id=1, source_target_pairs={{0,8},{8,16},{16,24},{24,0},{1,9},{9,17},{17,25},{25,1},{2,10},{10... | collective-permute-start | bytes 319496 | tf_op jit(solution)/shard_map/ppermute | solution.py:19
  130.0 4.3 copy-start.7
  130.0 4.3 copy-start.21
  130.0 4.3 copy-start.31
  130.0 4.5 copy-start.9
  130.0 196.1 %copy-start.11 = (bf16[4,13,13,16]{1,2,0,3:T(8,128)(2,1)}, bf16[4,13,13,16]{1,2,0,3:T(8,128)(2,1)S(1)}, u32[]{:S(2)}) copy-start(bf16[4,13,13,16]{1,2,0,3:T(8,128)(2,1)S(1)} %collective-permute-done.4) | copy-start | bytes 64900
  134.7 3.7 copy-start.1
  143.7 40.9 %collective-permute-start.6 = (bf16[1,2,13312]{2,1,0:T(2,128)(2,1)}, bf16[1,2,13312]{2,1,0:T(2,128)(2,1)}, u32[]{:S(2)}, u32[]{:S(2)}) collective-permute-start(bf16[1,2,13312]{2,1,0:T(2,128)(2,1)} %slice.731), channel_id=1, source_target_pairs={{0,32},{32,64},{64,96},{96,128},{128,160},{160,192},{192,224},{224... | collective-permute-start | bytes 159752 | tf_op jit(solution)/shard_map/ppermute | solution.py:19
  148.9 44.8 %collective-permute-start.7 = (bf16[1,2,13312]{2,1,0:T(2,128)(2,1)}, bf16[1,2,13312]{2,1,0:T(2,128)(2,1)}, u32[]{:S(2)}, u32[]{:S(2)}) collective-permute-start(bf16[1,2,13312]{2,1,0:T(2,128)(2,1)} %slice.744), channel_id=1, source_target_pairs={{32,0},{64,32},{96,64},{128,96},{160,128},{192,160},{224,192},{256... | collective-permute-start | bytes 159752 | tf_op jit(solution)/shard_map/ppermute | solution.py:22
  202.5 10.7 %collective-permute-start.8 = (bf16[4,1,13312]{2,1,0:T(2,128)(2,1)S(1)}, bf16[4,1,13312]{2,1,0:T(2,128)(2,1)S(1)}, u32[]{:S(2)}, u32[]{:S(2)}) collective-permute-start(bf16[4,1,13312]{2,1,0:T(2,128)(2,1)S(1)} %get-tuple-element.103), channel_id=1, source_target_pairs={{0,8},{8,16},{16,24},{24,0},{1,9},{9,17},{17,25},{25,1},{2,10},{10... | collective-permute-start | bytes 319496 | tf_op jit(solution)/shard_map/ppermute | solution.py:19
  204.4 19.9 %collective-permute-start.9 = (bf16[4,1,13312]{2,1,0:T(2,128)(2,1)}, bf16[4,1,13312]{2,1,0:T(2,128)(2,1)}, u32[]{:S(2)}, u32[]{:S(2)}) collective-permute-start(bf16[4,1,13312]{2,1,0:T(2,128)(2,1)} %get-tuple-element.104), channel_id=1, source_target_pairs={{8,0},{16,8},{24,16},{0,24},{9,1},{17,9},{25,17},{1,25},{10,2},{18... | collective-permute-start | bytes 319496 | tf_op jit(solution)/shard_map/ppermute | solution.py:22
  233.2 4.6 copy-start.2
  233.2 4.6 copy-start.10
  239.2 3.7 copy-start.5
  248.3 41.1 %collective-permute-start.10 = (bf16[1,2,13312]{2,1,0:T(2,128)(2,1)}, bf16[1,2,13312]{2,1,0:T(2,128)(2,1)}, u32[]{:S(2)}, u32[]{:S(2)}) collective-permute-start(bf16[1,2,13312]{2,1,0:T(2,128)(2,1)} %slice.779), channel_id=1, source_target_pairs={{0,32},{32,64},{64,96},{96,128},{128,160},{160,192},{192,224},{224... | collective-permute-start | bytes 159752 | tf_op jit(solution)/shard_map/ppermute | solution.py:19
  253.3 45.2 %collective-permute-start.11 = (bf16[1,2,13312]{2,1,0:T(2,128)(2,1)}, bf16[1,2,13312]{2,1,0:T(2,128)(2,1)}, u32[]{:S(2)}, u32[]{:S(2)}) collective-permute-start(bf16[1,2,13312]{2,1,0:T(2,128)(2,1)} %slice.792), channel_id=1, source_target_pairs={{32,0},{64,32},{96,64},{128,96},{160,128},{192,160},{224,192},{256... | collective-permute-start | bytes 159752 | tf_op jit(solution)/shard_map/ppermute | solution.py:22
  307.3 10.7 %collective-permute-start.12 = (bf16[4,1,13312]{2,1,0:T(2,128)(2,1)S(1)}, bf16[4,1,13312]{2,1,0:T(2,128)(2,1)S(1)}, u32[]{:S(2)}, u32[]{:S(2)}) collective-permute-start(bf16[4,1,13312]{2,1,0:T(2,128)(2,1)S(1)} %get-tuple-element.99), channel_id=1, source_target_pairs={{0,8},{8,16},{16,24},{24,0},{1,9},{9,17},{17,25},{25,1},{2,10},{10... | collective-permute-start | bytes 319496 | tf_op jit(solution)/shard_map/ppermute | solution.py:19
  309.2 19.3 %collective-permute-start.13 = (bf16[4,1,13312]{2,1,0:T(2,128)(2,1)}, bf16[4,1,13312]{2,1,0:T(2,128)(2,1)}, u32[]{:S(2)}, u32[]{:S(2)}) collective-permute-start(bf16[4,1,13312]{2,1,0:T(2,128)(2,1)} %get-tuple-element.100), channel_id=1, source_target_pairs={{8,0},{16,8},{24,16},{0,24},{9,1},{17,9},{25,17},{1,25},{10,2},{18... | collective-permute-start | bytes 319496 | tf_op jit(solution)/shard_map/ppermute | solution.py:22
  328.5 11.4 %copy-start.22 = (f32[13,64,16]{1,0,2:T(8,128)S(1)}, f32[13,64,16]{1,0,2:T(8,128)}, u32[]{:S(2)}) copy-start(f32[13,64,16]{1,0,2:T(8,128)} %fusion.137) | copy-start | bytes 159748
  337.4 4.5 copy-start.3
  337.4 4.5 copy-start.6
  346.2 4.8 slice-start
  351.0 329.8 %all-reduce.3.cloned.1.call-start = ((), (), s32[]{:S(2)}) async-start(), calls=%async_computation.1 | async-start | bytes 1048576
  352.5 33.6 %collective-permute-start.14 = (bf16[1,2,13312]{2,1,0:T(2,128)(2,1)}, bf16[1,2,13312]{2,1,0:T(2,128)(2,1)S(1)}, u32[]{:S(2)}, u32[]{:S(2)}) collective-permute-start(bf16[1,2,13312]{2,1,0:T(2,128)(2,1)} %slice.827), channel_id=1, source_target_pairs={{0,32},{32,64},{64,96},{96,128},{128,160},{160,192},{192,224},{224... | collective-permute-start | bytes 159752 | tf_op jit(solution)/shard_map/ppermute | solution.py:19
  355.8 32.6 %collective-permute-start.15 = (bf16[1,2,13312]{2,1,0:T(2,128)(2,1)}, bf16[1,2,13312]{2,1,0:T(2,128)(2,1)S(1)}, u32[]{:S(2)}, u32[]{:S(2)}) collective-permute-start(bf16[1,2,13312]{2,1,0:T(2,128)(2,1)} %slice.840), channel_id=1, source_target_pairs={{32,0},{64,32},{96,64},{128,96},{160,128},{192,160},{224,192},{256... | collective-permute-start | bytes 159752 | tf_op jit(solution)/shard_map/ppermute | solution.py:22
  371.4 9.2 %copy-start = (bf16[6,13,13,128]{2,1,0,3:T(8,128)(2,1)S(1)}, bf16[6,13,13,128]{2,1,0,3:T(8,128)(2,1)}, u32[]{:S(2)}) copy-start(bf16[6,13,13,128]{2,1,0,3:T(8,128)(2,1)} %copy.268) | copy-start | bytes 778756
  392.1 13.1 %copy-start.12 = (bf16[4,13,13,16]{1,2,0,3:T(8,128)(2,1)S(1)}, bf16[4,13,13,16]{1,2,0,3:T(8,128)(2,1)}, u32[]{:S(2)}) copy-start(bf16[4,13,13,16]{1,2,0,3:T(8,128)(2,1)} %copy-done.11) | copy-start | bytes 64900
  392.2 9.1 %collective-permute-start.16 = (bf16[4,1,13312]{2,1,0:T(2,128)(2,1)S(1)}, bf16[4,1,13312]{2,1,0:T(2,128)(2,1)S(1)}, u32[]{:S(2)}, u32[]{:S(2)}) collective-permute-start(bf16[4,1,13312]{2,1,0:T(2,128)(2,1)S(1)} %get-tuple-element.95), channel_id=1, source_target_pairs={{0,8},{8,16},{16,24},{24,0},{1,9},{9,17},{17,25},{25,1},{2,10},{10... | collective-permute-start | bytes 319496 | tf_op jit(solution)/shard_map/ppermute | solution.py:19
  394.2 11.5 %collective-permute-start.17 = (bf16[4,1,13312]{2,1,0:T(2,128)(2,1)S(1)}, bf16[4,1,13312]{2,1,0:T(2,128)(2,1)S(1)}, u32[]{:S(2)}, u32[]{:S(2)}) collective-permute-start(bf16[4,1,13312]{2,1,0:T(2,128)(2,1)S(1)} %get-tuple-element.96), channel_id=1, source_target_pairs={{8,0},{16,8},{24,16},{0,24},{9,1},{17,9},{25,17},{1,25},{10,2},{18... | collective-permute-start | bytes 319496 | tf_op jit(solution)/shard_map/ppermute | solution.py:22
  405.6 7.3 %copy-start.8 = (f32[13,64,128]{1,0,2:T(8,128)S(1)}, f32[13,64,128]{1,0,2:T(8,128)}, u32[]{:S(2)}) copy-start(f32[13,64,128]{1,0,2:T(8,128)} %fusion.12) | copy-start | bytes 1277956
  407.0 7.0 %copy-start.4 = (bf16[13,64,128]{1,0,2:T(8,128)(2,1)S(1)}, bf16[13,64,128]{1,0,2:T(8,128)(2,1)}, u32[]{:S(2)}) copy-start(bf16[13,64,128]{1,0,2:T(8,128)(2,1)} %fusion.32) | copy-start | bytes 638980
  411.5 2.7 copy-start.20
  (6 other events, 4.5 us)
Sparse Core Ops, SparseCore 0:
  351.1 26.1 all-gather.1
  419.5 261.1 all-reduce.2
where the time goes:
time: 696 us; the launch traced here: 689 us
  waiting for transfers between devices  264 us (38%)
  local copies, waits for them, and re-layouts  218 us (31%)
  matrix products  102 us (15%)
  starting transfers between devices  67.4 us (10%)
  other arithmetic  20.3 us (3%)
  between operations  18.1 us (3%)
    unnamed x3, waiting for transfers between devices  259 us
    ppermute x8, starting transfers between devices, padded(): lax.ppermute(lax.slice_in_dim(block, 0, width, axis=dim), axis, backward)  44 us
    dot_general x4, matrix products, interior(): jnp.einsum('pvkb,akb->pva', back_terms, choose_full, precision=lax.Precis...  34.9 us
    transpose x14, local copies, waits for them, and re-layouts, unpack(): return pieces.transpose(1, 2, 0, 3).reshape(orbitals, vec_width, edge_size)  32.9 us
    another operation x16, local copies, waits for them, and re-layouts, unpack(): layer.reshape(2, orbitals, vec_width, 2, group_size)[:, :, :, member]  31.9 us
    convert_element_type x4, local copies, waits for them, and re-layouts, interior(): gathered = jnp.einsum('ova,akb->pvkb'.replace('p', 'o'), source, choose_h...  25.5 us
    slice x8, local copies, waits for them, and re-layouts, unpack(): layer.reshape(2, orbitals, vec_width, 2, group_size)[:, :, :, member]  23.3 us
    unnamed x87, local copies, waits for them, and re-layouts  20.7 us
  transfers between devices with their start and end apart: 20, of which 2 were waited for; matrix products, arithmetic and copies ran while one was open for 36% of the time, Pallas kernels for 0%

commit v1 on v0

v1 whole, which is shorter than its diff:
```python
import functools

import jax
import jax.numpy as jnp
from jax import lax
from jax.experimental import pallas as pl
from jax.experimental.pallas import tpu as pltpu
from jax.sharding import PartitionSpec as P

MESH = pl.DeviceIdType.MESH
F32 = jnp.float32
BF16 = jnp.bfloat16
ORB = 13
VEC = 64
ATOMS = 128
SLOTS = 6
REACH = 4
EDGE = 16
WIDE = ORB * ATOMS
NZ = 16
NY = 4
HALF_A = 7


def strip_place(orbital, strip):
    return orbital // 8, ((4 + strip + orbital) % 8) * EDGE


def nt_dot(left, right):
    return lax.dot_general(left, right, (((1,), (1,)), ((), ())), preferred_element_type=F32)


def joined(ref, first, last):
    return jnp.concatenate([ref[o] for o in range(first, last)], axis=1)


def kernel(
    vec_in, pairs_in, count_in, blocks_in, cx_in, cy_in, top_ref, cut_ref,
    filt_out, corr_out, proj_out,
    field, pairs, count, blocks, cross, spread, gathered_rows, mask, inner, rim, rim_got,
    strips, strips_got, total, right_side, prev_got, next_got, far_got,
    ysend, ygot, zsend, zgot,
    load_sem, store_sem, rim_send, rim_recv, strip_send, strip_recv, ring_send, ring_recv,
    pair_send, pair_recv, y_send, y_recv, z_send, z_recv,
):
    dx, dy, band = lax.axis_index("dx"), lax.axis_index("dy"), lax.axis_index("band")
    chip, core = band // 2, band % 2
    east = ((dx + 1) % NZ, dy, band)
    west = ((dx + NZ - 1) % NZ, dy, band)
    north = (dx, (dy + 1) % NY, band)
    south = (dx, (dy + NY - 1) % NY, band)
    sibling = (dx, dy, 2 * chip + 1 - core)
    after = (dx, dy, 2 * ((chip + 1) % 4) + core)
    before = (dx, dy, 2 * ((chip + 3) % 4) + core)

    loads = [
        pltpu.make_async_copy(source, target, load_sem.at[index])
        for index, (source, target) in enumerate(
            (
                (vec_in, field.at[0]),
                (cx_in, cross.at[0]),
                (cy_in, cross.at[1]),
                (pairs_in, pairs),
                (count_in, count),
                (blocks_in, blocks),
            )
        )
    ]
    for load in loads:
        load.start()

    barrier = pltpu.get_barrier_semaphore()

    def greet(step, carry):
        pl.semaphore_signal(barrier, inc=1, device_id=((dx + step) % NZ, dy, band), device_id_type=MESH)
        return carry

    lax.fori_loop(1, NZ, greet, 0)
    for dj in range(NY):
        for dk in range(2):
            if dj or dk:
                pl.semaphore_signal(
                    barrier, inc=1,
                    device_id=(dx, (dy + dj) % NY, 2 * chip + (core + dk) % 2), device_id_type=MESH,
                )
    pl.semaphore_signal(barrier, inc=1, device_id=after, device_id_type=MESH)
    pl.semaphore_signal(barrier, inc=1, device_id=before, device_id_type=MESH)

    lane_group = lax.broadcasted_iota(jnp.int32, (VEC, ATOMS), 1) // EDGE

    def send_strips(step):
        for tile, (first, last) in enumerate(((0, 8), (8, ORB))):
            packed = [jnp.zeros((VEC, ATOMS), F32) for _ in range(4)]
            for o in range(first, last):
                turned = field[step, o].astype(F32)
                if o % 8:
                    turned = pltpu.roll(turned, EDGE * (o % 8), 1)
                for s in range(4):
                    packed[s] = jnp.where(lane_group == (4 + s + o) % 8, turned, packed[s])
            for s in range(4):
                strips[step, s, :, tile * ATOMS : (tile + 1) * ATOMS] = packed[s].astype(BF16)

    def strip_copies(step):
        return [
            pltpu.make_async_remote_copy(
                src_ref=strips.at[step, s], dst_ref=strips_got.at[step, s],
                send_sem=strip_send.at[step, s], recv_sem=strip_recv.at[step, s],
                device_id=target, device_id_type=MESH,
            )
            for s, target in enumerate((west, east, south, north))
        ]

    loads[0].wait()
    send_strips(0)

    loads[1].wait()
    loads[2].wait()
    spread[...] = jnp.zeros_like(spread)
    rim[...] = jnp.zeros_like(rim)
    edge_group = lax.broadcasted_iota(jnp.int32, (EDGE, ATOMS), 1) // EDGE
    edge_place = lax.broadcasted_iota(jnp.int32, (EDGE, ATOMS), 1) % EDGE
    edge_row = lax.broadcasted_iota(jnp.int32, (EDGE, ATOMS), 0)
    for axis in range(2):
        row_strip, col_strip = 2 * axis, 2 * axis + 1

        def spread_one(m, carry):
            for o in range(ORB):
                spread[o, 0:ORB, 0:EDGE] = cross[axis, m, o].astype(F32)
            for tile, (first, last) in enumerate(((0, 8), (8, ORB))):
                rows = jnp.zeros((EDGE, ATOMS), F32)
                for o in range(first, last):
                    _, lane = strip_place(o, col_strip)
                    turned = spread[o]
                    if lane:
                        turned = pltpu.roll(turned, lane, 1)
                    rows = jnp.where(edge_group == lane // EDGE, turned, rows)
                gathered_rows[m, :, tile * ATOMS : (tile + 1) * ATOMS] = rows
            return carry

        lax.fori_loop(0, REACH, spread_one, 0)
        for p in range(ORB):
            tile_row, lane_row = strip_place(p, row_strip)
            base = tile_row * ATOMS + lane_row
            for tile in range(2):
                block = jnp.zeros((EDGE, ATOMS), F32)
                for m in range(REACH):
                    line = gathered_rows[m, p : p + 1, tile * ATOMS : (tile + 1) * ATOMS]
                    block = jnp.where((edge_place + m) % EDGE == edge_row, line, block)
                rim[axis, base : base + EDGE, tile * ATOMS : (tile + 1) * ATOMS] = block.astype(BF16)

    pl.semaphore_wait(barrier, NZ - 1 + 2 * NY - 1 + 2)
    for copy in strip_copies(0):
        copy.start()
    rim_copies = [
        pltpu.make_async_remote_copy(
            src_ref=rim.at[axis], dst_ref=rim_got.at[axis],
            send_sem=rim_send.at[axis], recv_sem=rim_recv.at[axis],
            device_id=target, device_id_type=MESH,
        )
        for axis, target in enumerate((east, north))
    ]
    for copy in rim_copies:
        copy.start()

    for load in loads[3:]:
        load.wait()
    partner = lax.broadcasted_iota(jnp.int32, (ATOMS, ATOMS), 0)
    for k in range(SLOTS):
        chosen = jnp.where(k < count[...].reshape(1, ATOMS), pairs[k : k + 1, :], -1)
        mask[k] = jnp.where(partner == chosen, 1.0, 0.0).astype(BF16)

    def build(o, carry):
        for p in range(ORB):
            tile = mask[0] * blocks[0, o, p : p + 1, :]
            for k in range(1, SLOTS):
                tile = tile + mask[k] * blocks[k, o, p : p + 1, :]
            inner[p * ATOMS : (p + 1) * ATOMS, pl.ds(pl.multiple_of(o * ATOMS, ATOMS), ATOMS)] = tile
        return carry

    lax.fori_loop(0, ORB, build, 0)

    half = (jnp.full((1, ATOMS), top_ref[0], F32) - cut_ref[0]) * 0.5
    centre = (top_ref[0] + cut_ref[0]) * 0.5
    inverse = 1.0 / half
    upper = lane_group >= 4

    def interior(step):
        left = joined(field.at[step], 0, ORB)
        for g in range(7):
            first, last = 2 * g, min(2 * g + 2, ORB)
            part = jnp.dot(left, inner[:, first * ATOMS : last * ATOMS], preferred_element_type=F32)
            part = part + nt_dot(left, inner[first * ATOMS : last * ATOMS, :])
            for o in range(first, last):
                total[o] = part[:, (o - first) * ATOMS : (o - first + 1) * ATOMS]

    def finish(step, scale, keep):
        got = strips_got.at[step]
        from_east = jnp.dot(got[0], rim[0], preferred_element_type=F32)
        from_west = nt_dot(got[1], rim_got[0])
        from_north = jnp.dot(got[2], rim[1], preferred_element_type=F32)
        from_south = nt_dot(got[3], rim_got[1])
        added = (from_west, from_east, from_south, from_north)
        for o in range(ORB):
            tile = o // 8
            rows = jnp.zeros((VEC, ATOMS), F32)
            for s in range(4):
                rows = jnp.where(
                    lane_group == (4 + s + o) % 8, added[s][:, tile * ATOMS : (tile + 1) * ATOMS], rows
                )
            if o % 8:
                rows = pltpu.roll(rows, ATOMS - EDGE * (o % 8), 1)
            applied = total[o] + jnp.where(upper, rows, 0.0)
            result = (applied - centre * field[step, o].astype(F32)) * scale
            if keep is not None:
                result = result - field[keep, o].astype(F32)
            field[step + 1, o] = result.astype(BF16)

    own_rows = pl.ds(pl.multiple_of(core * 2 * VEC, 2 * VEC), VEC)
    own_image_rows = pl.ds(pl.multiple_of(core * 2 * VEC + VEC, VEC), VEC)

    def remote(source, target, send, recv, device):
        return pltpu.make_async_remote_copy(
            src_ref=source, dst_ref=target, send_sem=send, recv_sem=recv, device_id=device, device_id_type=MESH
        )

    part_a, part_b = pl.ds(0, HALF_A), pl.ds(HALF_A, ORB - HALF_A)
    ring_copies = [
        remote(field.at[3, part_a], prev_got.at[part_a], ring_send.at[0], ring_recv.at[0], after),
        remote(field.at[3, part_b], next_got.at[part_b], ring_send.at[1], ring_recv.at[1], before),
        remote(field.at[3, part_b], prev_got.at[part_b], ring_send.at[2], ring_recv.at[2], after),
        remote(field.at[3, part_a], next_got.at[part_a], ring_send.at[3], ring_recv.at[3], before),
        remote(prev_got.at[part_a], far_got.at[part_a], ring_send.at[4], ring_recv.at[4], after),
        remote(next_got.at[part_b], far_got.at[part_b], ring_send.at[5], ring_recv.at[5], before),
    ]
    pair_copies = [
        remote(field.at[3], right_side.at[:, own_rows], pair_send.at[0], pair_recv.at[0], sibling),
        remote(field.at[4], right_side.at[:, own_image_rows], pair_send.at[1], pair_recv.at[1], sibling),
    ]
    store = pltpu.make_async_copy(field.at[3], filt_out, store_sem)

    for step in range(4):
        if step:
            send_strips(step)
            for copy in strip_copies(step):
                copy.start()
        if step == 3:
            for copy in ring_copies[:4]:
                copy.start()
            pair_copies[0].start()
            store.start()
        interior(step)
        if step == 0:
            for copy in rim_copies:
                copy.wait_recv()
        if step == 3:
            ring_copies[0].wait_recv()
            ring_copies[4].start()
            ring_copies[1].wait_recv()
            ring_copies[5].start()
        for copy in strip_copies(step):
            copy.wait_recv()
        finish(step, inverse if step in (0, 3) else 2.0 * inverse, {1: 0, 2: 1}.get(step))

    pair_copies[1].start()
    for o in range(ORB):
        right_side[o, own_rows, :] = field[3, o]
        right_side[o, own_image_rows, :] = field[4, o]
    for copy in pair_copies:
        copy.wait_recv()

    def products(ref, offset):
        left = joined(ref, 0, ORB)
        right = joined(right_side, 0, ORB)
        result = nt_dot(left, right)
        rows = pl.ds(pl.multiple_of(((chip + offset) % 4) * 16, 16), 16)
        for j in range(NY):
            for k in range(2):
                lanes = slice(k * ATOMS, (k + 1) * ATOMS)
                piece = jnp.concatenate(
                    [result[8 * j : 8 * j + 8, lanes], result[32 + 8 * j : 40 + 8 * j, lanes]], axis=0
                )
                ysend[j, k, rows, :] = piece.astype(BF16)

    products(field.at[3], 0)
    ring_copies[2].wait_recv()
    products(prev_got, 3)
    ring_copies[3].wait_recv()
    products(next_got, 1)
    ring_copies[4].wait_recv()
    ring_copies[5].wait_recv()
    products(far_got, 2)

    y_copies = {}
    for dj, dk in ((2, 0), (2, 1), (1, 0), (3, 0), (1, 1), (3, 1), (0, 1)):
        to_y, to_core = (dy + dj) % NY, (core + dk) % 2
        slot = 2 * dj + dk
        y_copies[dj, dk] = remote(
            ysend.at[to_y, to_core], ygot.at[slot], y_send.at[slot], y_recv.at[slot],
            (dx, to_y, 2 * chip + to_core),
        )
        y_copies[dj, dk].start()
    for dk in range(2):
        summed = None
        for dj in (0, 1, 3, 2):
            if dj or dk:
                y_copies[dj, dk].wait_recv()
                term = ygot[2 * dj + dk].astype(F32)
            else:
                term = ysend[dy, core].astype(F32)
            summed = term if summed is None else summed + term
        from_core = (core + dk) % 2
        for c in range(4):
            for q in range(2):
                zsend[4 * c + 2 * from_core + q] = summed[16 * c + 8 * q : 16 * c + 8 * q + 8, :]

    def z_copy(step):
        target = (dx + step) % NZ
        return remote(zsend.at[target], zgot.at[step], z_send.at[step], z_recv.at[step], (target, dy, band))

    def z_start(step, carry):
        z_copy(step).start()
        return carry

    lax.fori_loop(1, NZ, z_start, 0)

    def z_take(step, value):
        z_copy(step).wait_recv()
        return value + zgot[step]

    final = lax.fori_loop(1, NZ, z_take, zsend[dx]) * (1.0 / (ORB * ATOMS * NZ * NY))
    turned = jnp.transpose(final)
    corr_out[...] = turned[0:VEC, :]
    proj_out[...] = turned[VEC:, :]

    def z_end(step, carry):
        z_copy(step).wait_send()
        return carry

    lax.fori_loop(1, NZ, z_end, 0)
    for step in range(4):
        for copy in strip_copies(step):
            copy.wait_send()
    for copy in rim_copies + ring_copies + pair_copies + list(y_copies.values()):
        copy.wait_send()
    store.wait()


def on_device(vectors, inner_pairs, inner_count, inner_blocks, cross_x_blocks, cross_y_blocks, spectrum_top, filter_cut):
    any_spec = pl.BlockSpec(memory_space=pl.ANY)
    vmem_spec = pl.BlockSpec(memory_space=pltpu.VMEM)
    smem_spec = pl.BlockSpec(memory_space=pltpu.SMEM)
    dma = pltpu.SemaphoreType.DMA
    small = jax.ShapeDtypeStruct((VEC, 8), F32)
    return pl.pallas_call(
        kernel,
        out_shape=(jax.ShapeDtypeStruct((ORB, VEC, ATOMS), BF16), small, small),
        in_specs=[any_spec] * 6 + [smem_spec] * 2,
        out_specs=(any_spec, vmem_spec, vmem_spec),
        scratch_shapes=[
            pltpu.VMEM((5, ORB, VEC, ATOMS), BF16),
            pltpu.VMEM((SLOTS, ATOMS), jnp.int32),
            pltpu.VMEM((ATOMS,), jnp.int32),
            pltpu.VMEM((SLOTS, ORB, ORB, ATOMS), BF16),
            pltpu.VMEM((2, REACH, ORB, ORB, EDGE), BF16),
            pltpu.VMEM((ORB, EDGE, ATOMS), F32),
            pltpu.VMEM((REACH, EDGE, 2 * ATOMS), F32),
            pltpu.VMEM((SLOTS, ATOMS, ATOMS), BF16),
            pltpu.VMEM((WIDE, WIDE), BF16),
            pltpu.VMEM((2, 2 * ATOMS, 2 * ATOMS), BF16),
            pltpu.VMEM((2, 2 * ATOMS, 2 * ATOMS), BF16),
            pltpu.VMEM((4, 4, VEC, 2 * ATOMS), BF16),
            pltpu.VMEM((4, 4, VEC, 2 * ATOMS), BF16),
            pltpu.VMEM((ORB, VEC, ATOMS), F32),
            pltpu.VMEM((ORB, 4 * VEC, ATOMS), BF16),
            pltpu.VMEM((ORB, VEC, ATOMS), BF16),
            pltpu.VMEM((ORB, VEC, ATOMS), BF16),
            pltpu.VMEM((ORB, VEC, ATOMS), BF16),
            pltpu.VMEM((NY, 2, VEC, ATOMS), BF16),
            pltpu.VMEM((2 * NY, VEC, ATOMS), BF16),
            pltpu.VMEM((NZ, 8, ATOMS), F32),
            pltpu.VMEM((NZ, 8, ATOMS), F32),
            dma((6,)), dma(()), dma((2,)), dma((2,)), dma((4, 4)), dma((4, 4)), dma((6,)), dma((6,)),
            dma((2,)), dma((2,)), dma((2 * NY,)), dma((2 * NY,)), dma((NZ,)), dma((NZ,)),
        ],
        compiler_params=pltpu.CompilerParams(
            collective_id=0, has_side_effects=True, vmem_limit_bytes=48 * 1024 * 1024
        ),
        name="chebyshev",
    )(vectors, inner_pairs, inner_count, inner_blocks, cross_x_blocks, cross_y_blocks, spectrum_top, filter_cut)


def solution(mesh):
    in_specs = (
        P(None, "band", ("dx", "dy")),
        P(None, ("dx", "dy")),
        P(("dx", "dy")),
        P(None, None, None, ("dx", "dy")),
        P(None, None, None, ("dx", "dy")),
        P(None, None, None, ("dx", "dy")),
        P(),
        P(),
    )
    out_specs = (P(None, "band", ("dx", "dy")), P("band", ("dx", "dy")), P("band", ("dx", "dy")))
    return jax.shard_map(on_device, mesh=mesh, in_specs=in_specs, out_specs=out_specs, check_vma=False)
```

time: 696 us -> 60.6 us (0.09)
  waiting for transfers between devices: 264 us -> 0 us
  local copies, waits for them, and re-layouts: 218 us -> 4.04 us
  matrix products: 102 us -> 0 us
  starting transfers between devices: 67.4 us -> 0 us
  Pallas kernels: 0 us -> 53.9 us
  other arithmetic: 20.3 us -> 0 us
  between operations: 18.1 us -> 2 us
    unnamed x3 -> x0, waiting for transfers between devices: 259 us -> none
    dot_general x34 -> x0, matrix products: 102 us -> none  [the longest x4 34.9 us: interior(): jnp.einsum('pvkb,akb->pva', back_terms, choose_full, precision=lax.Precis...]
    ppermute x18 -> x0, starting transfers between devices: 67.3 us -> none  [the longest x8 44 us: padded(): lax.ppermute(lax.slice_in_dim(block, 0, width, axis=dim), axis, backward)]
    slice x145 -> x0, local copies, waits for them, and re-layouts: 63.3 us -> none  [the longest x8 23.3 us: unpack(): layer.reshape(2, orbitals, vec_width, 2, group_size)[:, :, :, member]]
    pallas_call x0 -> x1, Pallas kernels: none -> 53.9 us  [on_device(): pl.pallas_call(kernel, out_shape=(jax.ShapeDtypeStruct((ORB, VEC, ATOMS),...]
    transpose x18 -> x0, local copies, waits for them, and re-layouts: 39.8 us -> none  [the longest x14 32.9 us: unpack(): return pieces.transpose(1, 2, 0, 3).reshape(orbitals, vec_width, edge_size)]
    another operation x19 -> x0, local copies, waits for them, and re-layouts: 36.4 us -> none  [the longest x16 31.9 us: unpack(): layer.reshape(2, orbitals, vec_width, 2, group_size)[:, :, :, member]]
    convert_element_type x4 -> x0, local copies, waits for them, and re-layouts: 25.5 us -> none  [interior(): gathered = jnp.einsum('ova,akb->pvkb'.replace('p', 'o'), source, choose_h...]
  transfers between devices with their start and end apart: 20 -> 0, of which waited for: 2 -> 0; matrix products, arithmetic and copies ran while one was open for 36% -> 0% of each run, Pallas kernels for 0% -> 0%
where the time goes in v1:
time: 60.6 us; the launch traced here: 60 us
  Pallas kernels  53.9 us (89%)
  local copies, waits for them, and re-layouts  4.04 us (7%)
  between operations  2 us (3%)
    pallas_call x1, Pallas kernels, on_device(): pl.pallas_call(kernel, out_shape=(jax.ShapeDtypeStruct((ORB, VEC, ATOMS),...  53.9 us
    unnamed x11, local copies, waits for them, and re-layouts  2.72 us
    pallas_call x2, local copies, waits for them, and re-layouts, on_device(): pl.pallas_call(kernel, out_shape=(jax.ShapeDtypeStruct((ORB, VEC, ATOMS),...  1.32 us

profile of v1, /device:TPU:6, one launch (start us, length us, event | category | flops | bytes accessed | tf_op | source)
XLA Modules:
  0.0 60.0 jit_solution(8757817117018609176)
XLA Ops:
  1.9 0.0 copy-start
  1.9 1.0 %copy.11.cx_in = bf16[4,13,13,16]{3,2,1,0:T(8,128)(2,1)S(1)} copy(bf16[4,13,13,16]{3,0,2,1:T(4,128)(2,1)} %param.12) | data formatting | bytes 43264 | tf_op args[4]
  2.9 0.0 copy-start.1
  3.0 0.0 copy-start.2
  3.0 0.0 copy-start.3
  3.0 1.0 %copy.12.cy_in = bf16[4,13,13,16]{3,2,1,0:T(8,128)(2,1)S(1)} copy(bf16[4,13,13,16]{3,0,2,1:T(4,128)(2,1)} %param.13) | data formatting | bytes 43264 | tf_op args[5]
  4.0 0.0 copy-done
  4.0 0.0 copy-done.1
  4.0 0.0 copy-done.2
  4.0 0.0 copy-done.3
  4.0 53.9 %chebyshev.1 = (bf16[13,64,128]{2,1,0:T(8,128)(2,1)S(1)}, f32[64,8]{1,0:T(8,128)S(1)}, f32[64,8]{1,0:T(8,128)S(1)}) custom-call(bf16[13,64,128]{2,1,0:T(8,128)(2,1)S(1)} %copy-done.1, s32[6,128]{1,0:T(8,128)S(1)} %copy-done.2, s32[128]{0:T(128)S(1)} %copy-done.3, bf16[6,13,13,128]{3,2,1,0:T(8,128)(2,1)S(1)} %copy-done, ...), custom_call_target="tpu_custom_call" | custom-call | tf_op jit(solution)/shard_map/chebyshev/pallas_call | solution.py:354
  58.0 0.7 %copy.13 = f32[64,8]{0,1:T(8,128)} copy(f32[64,8]{1,0:T(8,128)S(1)} %get-tuple-element.4) | data formatting | bytes 4096 | tf_op jit(solution)/shard_map/chebyshev/pallas_call | solution.py:354
  58.7 0.7 %copy.14 = f32[64,8]{0,1:T(8,128)} copy(f32[64,8]{1,0:T(8,128)S(1)} %get-tuple-element.5) | data formatting | bytes 4096 | tf_op jit(solution)/shard_map/chebyshev/pallas_call | solution.py:354
  59.3 0.7 %copy.18 = bf16[13,64,128]{2,1,0:T(8,128)(2,1)} copy(bf16[13,64,128]{2,1,0:T(8,128)(2,1)S(1)} %get-tuple-element.9) | data formatting | bytes 425984
Async XLA Ops:
  1.9 2.1 %copy-start = (bf16[6,13,13,128]{3,2,1,0:T(8,128)(2,1)S(1)}, bf16[6,13,13,128]{3,2,1,0:T(8,128)(2,1)}, u32[]{:S(2)}) copy-start(bf16[6,13,13,128]{3,2,1,0:T(8,128)(2,1)} %blocks_in.1) | copy-start | bytes 778756
  2.9 1.1 %copy-start.1 = (bf16[13,64,128]{2,1,0:T(8,128)(2,1)S(1)}, bf16[13,64,128]{2,1,0:T(8,128)(2,1)}, u32[]{:S(2)}) copy-start(bf16[13,64,128]{2,1,0:T(8,128)(2,1)} %vec_in.1) | copy-start | bytes 638980
  3.0 1.1 %copy-start.2 = (s32[6,128]{1,0:T(8,128)S(1)}, s32[6,128]{1,0:T(8,128)}, u32[]{:S(2)}) copy-start(s32[6,128]{1,0:T(8,128)} %pairs_in.1) | copy-start | bytes 9220
  3.0 1.1 %copy-start.3 = (s32[128]{0:T(128)S(1)}, s32[128]{0:T(128)}, u32[]{:S(2)}) copy-start(s32[128]{0:T(128)} %count_in.1) | copy-start | bytes 1540

commit v2 on v1

v2 whole, which is shorter than its diff:
```python
import functools

import jax
import jax.numpy as jnp
from jax import lax
from jax.experimental import pallas as pl
from jax.experimental.pallas import tpu as pltpu
from jax.sharding import PartitionSpec as P

MESH = pl.DeviceIdType.MESH
F32 = jnp.float32
BF16 = jnp.bfloat16
ORB = 13
VEC = 64
ATOMS = 128
SLOTS = 6
REACH = 4
EDGE = 16
WIDE = ORB * ATOMS
NZ = 16
VMEM_BYTES = 56 * 1024 * 1024
NY = 4


def nt_dot(left, right):
    return lax.dot_general(left, right, (((1,), (1,)), ((), ())), preferred_element_type=F32)


def joined(ref, first, last):
    return jnp.concatenate([ref[o] for o in range(first, last)], axis=1)


def kernel(
    vec_in, pairs_in, count_in, blocks_in, cx_in, cy_in, top_ref, cut_ref,
    filt_out, sums_out,
    field, pairs, count, blocks, cross, spread, chosen, double, lines, inner, whole, rim, rim_got, rim_lines, rim_sent, rim_came,
    strips, strips_got, total, inside, added, right_side, prev_got, next_got, far_got,
    ysend, ygot, zsend, zgot,
    load_sem, store_sem, rim_send, rim_recv, strip_send, strip_recv, ring_send, ring_recv,
    pair_send, pair_recv, y_send, y_recv, z_send, z_recv,
):
    dx, dy, band = lax.axis_index("dx"), lax.axis_index("dy"), lax.axis_index("band")
    chip, core = band // 2, band % 2
    east = ((dx + 1) % NZ, dy, band)
    west = ((dx + NZ - 1) % NZ, dy, band)
    north = (dx, (dy + 1) % NY, band)
    south = (dx, (dy + NY - 1) % NY, band)
    sibling = (dx, dy, 2 * chip + 1 - core)
    after = (dx, dy, 2 * ((chip + 1) % 4) + core)
    before = (dx, dy, 2 * ((chip + 3) % 4) + core)

    loads = [
        pltpu.make_async_copy(source, target, load_sem.at[index])
        for index, (source, target) in enumerate(
            (
                (vec_in, field.at[0]),
                (cx_in, cross.at[0]),
                (cy_in, cross.at[1]),
                (pairs_in, pairs),
                (count_in, count),
                (blocks_in, blocks),
            )
        )
    ]
    for load in loads:
        load.start()

    barrier = pltpu.get_barrier_semaphore()

    def greet(step, carry):
        pl.semaphore_signal(barrier, inc=1, device_id=((dx + step) % NZ, dy, band), device_id_type=MESH)
        return carry

    lax.fori_loop(1, NZ, greet, 0)
    for dj in range(NY):
        for dk in range(2):
            if dj or dk:
                pl.semaphore_signal(
                    barrier, inc=1,
                    device_id=(dx, (dy + dj) % NY, 2 * chip + (core + dk) % 2), device_id_type=MESH,
                )
    pl.semaphore_signal(barrier, inc=1, device_id=after, device_id_type=MESH)
    pl.semaphore_signal(barrier, inc=1, device_id=before, device_id_type=MESH)

    lane_group = lax.broadcasted_iota(jnp.int32, (VEC, ATOMS), 1) // EDGE

    def pack(source, target):
        for tile, (first, last) in enumerate(((0, 8), (8, ORB))):
            packed = [jnp.zeros((VEC, ATOMS), F32) for _ in range(4)]
            for o in range(first, last):
                turned = source[o].astype(F32)
                if o % 8:
                    turned = pltpu.roll(turned, EDGE * (o % 8), 1)
                for s in range(4):
                    packed[s] = jnp.where(lane_group == (4 + s + o) % 8, turned, packed[s])
            for s in range(4):
                target[s, :, tile * ATOMS : (tile + 1) * ATOMS] = packed[s].astype(target.dtype)

    def strip_copies(step):
        return [
            pltpu.make_async_remote_copy(
                src_ref=strips.at[step, s], dst_ref=strips_got.at[step, s],
                send_sem=strip_send.at[step, s], recv_sem=strip_recv.at[step, s],
                device_id=target, device_id_type=MESH,
            )
            for s, target in enumerate((west, east, south, north))
        ]

    loads[0].wait()
    pack(field.at[0], strips.at[0])

    loads[1].wait()
    loads[2].wait()
    spread[...] = jnp.zeros_like(spread)
    rim[...] = jnp.zeros_like(rim)
    rim_got[...] = jnp.zeros_like(rim_got)
    rim_lines[...] = jnp.zeros_like(rim_lines)
    line_group = lax.broadcasted_iota(jnp.int32, (8, ATOMS), 1) // EDGE
    edge_place = lax.broadcasted_iota(jnp.int32, (EDGE, ATOMS), 1) % EDGE
    edge_row = lax.broadcasted_iota(jnp.int32, (EDGE, ATOMS), 0)
    edge_hits = [(edge_place + m) % EDGE == edge_row for m in range(REACH)]
    for axis in range(2):
        col_strip = 2 * axis + 1

        spread[:, :, 0:REACH, 0:EDGE] = cross[axis].astype(F32)
        for p in range(ORB):
            for tile, (first, last) in enumerate(((0, 8), (8, ORB))):
                packed = jnp.zeros((8, ATOMS), F32)
                for o in range(first, last):
                    group = (4 + col_strip + o) % 8
                    turned = spread[o, p]
                    if group:
                        turned = pltpu.roll(turned, group * EDGE, 1)
                    packed = jnp.where(line_group == group, turned, packed)
                rim_lines[axis, REACH * p : REACH * (p + 1), tile * ATOMS : (tile + 1) * ATOMS] = packed[0:REACH, :]
        rim_sent[axis] = rim_lines[axis].astype(BF16)

    def widen(axis, target):
        for p in range(ORB):
            place = (p // 8) * ATOMS + ((4 + 2 * axis + p) % 8) * EDGE
            for tile in range(2):
                lanes = slice(tile * ATOMS, (tile + 1) * ATOMS)
                block = jnp.zeros((EDGE, ATOMS), F32)
                for m in range(REACH):
                    line = REACH * p + m
                    block = jnp.where(edge_hits[m], rim_lines[axis, line : line + 1, lanes], block)
                target[axis, place : place + EDGE, lanes] = block.astype(BF16)

    for load in loads[3:]:
        load.wait()
    taken = []
    for k in range(SLOTS):
        here = jnp.where(k < count[...].reshape(1, ATOMS), pairs[k : k + 1, :], -1)
        seen = jnp.zeros((1, ATOMS), F32)
        for earlier in range(k):
            same = jnp.where((taken[earlier] == here) & (here >= 0), 1.0, 0.0)
            double[k, earlier : earlier + 1, :] = same
            seen = seen + same
        taken.append(jnp.where(seen > 0.5, -1, here))
        chosen[k : k + 1, :] = taken[k]
    partner = lax.broadcasted_iota(jnp.int32, (EDGE, ATOMS), 0)

    def build(o, carry):
        merged = [blocks[k, o].astype(F32) for k in range(SLOTS)]
        for k in range(1, SLOTS):
            for earlier in range(k):
                merged[earlier] = merged[earlier] + merged[k] * double[k, earlier : earlier + 1, :]
        for k in range(SLOTS):
            lines[k, 0:ORB, :] = merged[k]
        columns = pl.ds(pl.multiple_of(o * ATOMS, ATOMS), ATOMS)
        for start in range(0, ATOMS, EDGE):
            hits = [partner + start == chosen[k : k + 1, :] for k in range(SLOTS)]
            for p in range(ORB):
                piece = jnp.zeros((EDGE, ATOMS), F32)
                for k in range(SLOTS):
                    piece = jnp.where(hits[k], lines[k, p : p + 1, :], piece)
                inner[p * ATOMS + start : p * ATOMS + start + EDGE, columns] = piece.astype(BF16)
        return carry

    lax.fori_loop(0, 7, build, 0)
    pl.semaphore_wait(barrier, NZ - 1 + 2 * NY - 1 + 2)
    rim_copies = [
        pltpu.make_async_remote_copy(
            src_ref=rim_sent.at[axis], dst_ref=rim_came.at[axis],
            send_sem=rim_send.at[axis], recv_sem=rim_recv.at[axis],
            device_id=target, device_id_type=MESH,
        )
        for axis, target in enumerate((east, north))
    ]
    for copy in rim_copies:
        copy.start()
    for copy in strip_copies(0):
        copy.start()
    for axis in range(2):
        widen(axis, rim)
    lax.fori_loop(7, ORB, build, 0)

    half = (jnp.full((1, ATOMS), top_ref[0], F32) - cut_ref[0]) * 0.5
    centre = (top_ref[0] + cut_ref[0]) * 0.5
    inverse = 1.0 / half
    wide_centre = jnp.full((1, 2 * ATOMS), centre, F32)
    wide_inverse = jnp.concatenate([inverse, inverse], axis=1)
    upper = lane_group >= 4

    def interior(step):
        left = joined(field.at[step], 0, ORB)
        for g in range(7):
            first, last = 2 * g, min(2 * g + 2, ORB)
            lanes = slice(first * ATOMS, last * ATOMS)
            if step == 0:
                for q in range(ORB):
                    rows = slice(q * ATOMS, (q + 1) * ATOMS)
                    whole[rows, lanes] = inner[rows, lanes] + jnp.transpose(inner[lanes, rows])
            part = jnp.dot(left, whole[:, lanes], preferred_element_type=F32)
            for o in range(first, last):
                total[o] = part[:, (o - first) * ATOMS : (o - first + 1) * ATOMS]

    def advance(step, s, scale, keep):
        source = (1, 0, 3, 2)[s]
        strip_copies(step)[source].wait_recv()
        got = strips_got[step, source]
        across = (
            jnp.dot(got, rim[s // 2], preferred_element_type=F32) if s % 2 else nt_dot(got, rim_got[s // 2])
        )
        added[s] = across
        if step < 3:
            result = (inside[s] + across - wide_centre * strips[step, s].astype(F32)) * scale
            if keep is not None:
                result = result - strips[keep, s].astype(F32)
            strips[step + 1, s] = result.astype(BF16)
            strip_copies(step + 1)[s].start()

    def finish(step, scale, keep):
        for o in range(ORB):
            tile = o // 8
            rows = jnp.zeros((VEC, ATOMS), F32)
            for s in range(4):
                rows = jnp.where(
                    lane_group == (4 + s + o) % 8, added[s, :, tile * ATOMS : (tile + 1) * ATOMS], rows
                )
            if o % 8:
                rows = pltpu.roll(rows, ATOMS - EDGE * (o % 8), 1)
            applied = total[o] + jnp.where(upper, rows, 0.0)
            result = (applied - centre * field[step, o].astype(F32)) * scale
            if keep is not None:
                result = result - field[keep, o].astype(F32)
            field[step + 1, o] = result.astype(BF16)

    own_rows = pl.ds(pl.multiple_of(core * 2 * VEC, 2 * VEC), VEC)
    own_image_rows = pl.ds(pl.multiple_of(core * 2 * VEC + VEC, VEC), VEC)

    def remote(source, target, send, recv, device):
        return pltpu.make_async_remote_copy(
            src_ref=source, dst_ref=target, send_sem=send, recv_sem=recv, device_id=device, device_id_type=MESH
        )

    def ring_copy(index, source, target, first, last, device):
        part = pl.ds(first, last - first)
        return remote(source.at[part], target.at[part], ring_send.at[index], ring_recv.at[index], device)

    mine = field.at[3]
    ring_copies = [
        ring_copy(0, mine, prev_got, 0, 4, after),
        ring_copy(1, mine, next_got, 7, 10, before),
        ring_copy(2, mine, prev_got, 4, 7, after),
        ring_copy(3, mine, next_got, 10, 13, before),
        ring_copy(4, mine, prev_got, 7, 13, after),
        ring_copy(5, mine, next_got, 0, 7, before),
    ]
    passed_on = [
        ring_copy(6, prev_got, far_got, 0, 4, after),
        ring_copy(7, next_got, far_got, 7, 10, before),
        ring_copy(8, prev_got, far_got, 4, 7, after),
        ring_copy(9, next_got, far_got, 10, 13, before),
    ]

    def pass_on(index):
        ring_copies[index].wait_recv()
        passed_on[index].start()

    pair_copies = [
        remote(field.at[3], right_side.at[:, own_rows], pair_send.at[0], pair_recv.at[0], sibling),
        remote(field.at[4], right_side.at[:, own_image_rows], pair_send.at[1], pair_recv.at[1], sibling),
    ]

    store = pltpu.make_async_copy(field.at[3], filt_out, store_sem)
    for step in range(4):
        keep = {1: 0, 2: 1}.get(step)
        factor = 1.0 if step in (0, 3) else 2.0
        if step == 3:
            for copy in ring_copies:
                copy.start()
            pair_copies[0].start()
            store.start()
        interior(step)
        if step < 3:
            pack(total, inside)
        if step == 0:
            for axis in range(2):
                rim_copies[axis].wait_recv()
                rim_lines[axis] = rim_came[axis].astype(F32)
                widen(axis, rim_got)
        if step == 3:
            pass_on(0)
            pass_on(1)
        for s in range(4):
            advance(step, s, wide_inverse * factor, keep)
        finish(step, inverse * factor, keep)

    pair_copies[1].start()
    pass_on(2)
    pass_on(3)
    for o in range(ORB):
        right_side[o, own_rows, :] = field[3, o]
        right_side[o, own_image_rows, :] = field[4, o]
    for copy in pair_copies:
        copy.wait_recv()

    def products(ref, turn):
        left = joined(ref, 0, ORB)
        right = joined(right_side, 0, ORB)
        result = nt_dot(left, right)
        rows = slice(16 * turn, 16 * turn + 16)
        for j in range(NY):
            for k in range(2):
                lanes = slice(k * ATOMS, (k + 1) * ATOMS)
                piece = jnp.concatenate(
                    [result[8 * j : 8 * j + 8, lanes], result[32 + 8 * j : 40 + 8 * j, lanes]], axis=0
                )
                ysend[j, k, rows, :] = piece.astype(BF16)

    y_copies = []

    def y_start(part, first, last):
        rows = pl.ds(first, last - first)
        for dj, dk in ((2, 0), (2, 1), (1, 0), (3, 0), (1, 1), (3, 1), (0, 1)):
            to_y, to_core = (dy + dj) % NY, (core + dk) % 2
            slot = 2 * dj + dk
            copy = remote(
                ysend.at[to_y, to_core, rows], ygot.at[slot, rows], y_send.at[part, slot], y_recv.at[part, slot],
                (dx, to_y, 2 * chip + to_core),
            )
            copy.start()
            y_copies.append(copy)

    products(field.at[3], 0)
    ring_copies[4].wait_recv()
    products(prev_got, 1)
    ring_copies[5].wait_recv()
    products(next_got, 2)
    y_start(0, 0, 48)
    for copy in passed_on:
        copy.wait_recv()
    products(far_got, 3)
    y_start(1, 48, 64)
    for copy in y_copies:
        copy.wait_recv()
    for dk in range(2):
        summed = ygot[dk].astype(F32) if dk else ysend[dy, core].astype(F32)
        for dj in (1, 3, 2):
            summed = summed + ygot[2 * dj + dk].astype(F32)
        from_core = (core + dk) % 2
        for turn, offset in enumerate((0, 3, 1, 2)):
            for q in range(2):
                place = 4 * ((chip + offset) % 4) + 2 * from_core + q
                zsend[place] = summed[16 * turn + 8 * q : 16 * turn + 8 * q + 8, :]

    def z_copy(step):
        target = (dx + step) % NZ
        return remote(zsend.at[target], zgot.at[step], z_send.at[step], z_recv.at[step], (target, dy, band))

    def z_start(index, carry):
        z_copy(NZ // 2 + (index + 1) // 2 * (1 - 2 * (index % 2))).start()
        return carry

    lax.fori_loop(0, NZ - 1, z_start, 0)

    def z_take(step, value):
        z_copy(step).wait_recv()
        return value + zgot[step]

    final = lax.fori_loop(1, NZ, z_take, zsend[dx]) * (1.0 / (ORB * ATOMS * NZ * NY))
    sums_out[...] = final

    def z_end(step, carry):
        z_copy(step).wait_send()
        return carry

    lax.fori_loop(1, NZ, z_end, 0)
    for step in range(4):
        for copy in strip_copies(step):
            copy.wait_send()
    for copy in rim_copies + ring_copies + passed_on + pair_copies + y_copies:
        copy.wait_send()
    store.wait()


def hand_over(filtered, sums, filt_out, corr_out, proj_out, sem):
    copy = pltpu.make_async_copy(filtered, filt_out, sem)
    copy.start()
    corr_out[...] = sums[:, 0:VEC]
    proj_out[...] = sums[:, VEC:]
    copy.wait()


def on_device(vectors, inner_pairs, inner_count, inner_blocks, cross_x_blocks, cross_y_blocks, spectrum_top, filter_cut):
    any_spec = pl.BlockSpec(memory_space=pl.ANY)
    hbm_spec = pl.BlockSpec(memory_space=pltpu.HBM)
    vmem_spec = pl.BlockSpec(memory_space=pltpu.VMEM)
    smem_spec = pl.BlockSpec(memory_space=pltpu.SMEM)
    dma = pltpu.SemaphoreType.DMA
    block = jax.ShapeDtypeStruct((ORB, VEC, ATOMS), BF16)
    small = jax.ShapeDtypeStruct((8, VEC), F32)
    filtered, sums = pl.pallas_call(
        kernel,
        out_shape=(block, jax.ShapeDtypeStruct((8, ATOMS), F32)),
        in_specs=[hbm_spec] * 6 + [smem_spec] * 2,
        out_specs=(any_spec, vmem_spec),
        scratch_shapes=[
            pltpu.VMEM((5, ORB, VEC, ATOMS), BF16),
            pltpu.VMEM((SLOTS, ATOMS), jnp.int32),
            pltpu.VMEM((ATOMS,), jnp.int32),
            pltpu.VMEM((SLOTS, ORB, ORB, ATOMS), BF16),
            pltpu.VMEM((2, ORB, ORB, REACH, EDGE), BF16),
            pltpu.VMEM((ORB, ORB, 8, ATOMS), F32),
            pltpu.VMEM((8, ATOMS), jnp.int32),
            pltpu.VMEM((SLOTS, 8, ATOMS), F32),
            pltpu.VMEM((SLOTS, EDGE, ATOMS), F32),
            pltpu.VMEM((WIDE, WIDE), BF16),
            pltpu.VMEM((WIDE, WIDE), BF16),
            pltpu.VMEM((2, 2 * ATOMS, 2 * ATOMS), BF16),
            pltpu.VMEM((2, 2 * ATOMS, 2 * ATOMS), BF16),
            pltpu.VMEM((2, VEC, 2 * ATOMS), F32),
            pltpu.VMEM((2, VEC, 2 * ATOMS), BF16),
            pltpu.VMEM((2, VEC, 2 * ATOMS), BF16),
            pltpu.VMEM((4, 4, VEC, 2 * ATOMS), BF16),
            pltpu.VMEM((4, 4, VEC, 2 * ATOMS), BF16),
            pltpu.VMEM((ORB, VEC, ATOMS), F32),
            pltpu.VMEM((4, VEC, 2 * ATOMS), F32),
            pltpu.VMEM((4, VEC, 2 * ATOMS), F32),
            pltpu.VMEM((ORB, 4 * VEC, ATOMS), BF16),
            pltpu.VMEM((ORB, VEC, ATOMS), BF16),
            pltpu.VMEM((ORB, VEC, ATOMS), BF16),
            pltpu.VMEM((ORB, VEC, ATOMS), BF16),
            pltpu.VMEM((NY, 2, VEC, ATOMS), BF16),
            pltpu.VMEM((2 * NY, VEC, ATOMS), BF16),
            pltpu.VMEM((NZ, 8, ATOMS), F32),
            pltpu.VMEM((NZ, 8, ATOMS), F32),
            dma((6,)), dma(()), dma((2,)), dma((2,)), dma((4, 4)), dma((4, 4)), dma((10,)), dma((10,)),
            dma((2,)), dma((2,)), dma((2, 2 * NY)), dma((2, 2 * NY)), dma((NZ,)), dma((NZ,)),
        ],
        compiler_params=pltpu.CompilerParams(
            collective_id=0, has_side_effects=True, vmem_limit_bytes=VMEM_BYTES
        ),
        name="chebyshev",
    )(
        vectors, inner_pairs, inner_count, inner_blocks,
        cross_x_blocks.transpose(1, 2, 0, 3), cross_y_blocks.transpose(1, 2, 0, 3), spectrum_top, filter_cut,
    )
    filtered, correlation, projected = pl.pallas_call(
        hand_over,
        out_shape=(block, small, small),
        in_specs=[vmem_spec, vmem_spec],
        out_specs=(any_spec, vmem_spec, vmem_spec),
        scratch_shapes=[dma(())],
        compiler_params=pltpu.CompilerParams(vmem_limit_bytes=VMEM_BYTES),
        name="hand_over",
    )(filtered, sums)
    return filtered, correlation.T, projected.T


def solution(mesh):
    in_specs = (
        P(None, "band", ("dx", "dy")),
        P(None, ("dx", "dy")),
        P(("dx", "dy")),
        P(None, None, None, ("dx", "dy")),
        P(None, None, None, ("dx", "dy")),
        P(None, None, None, ("dx", "dy")),
        P(),
        P(),
    )
    out_specs = (P(None, "band", ("dx", "dy")), P("band", ("dx", "dy")), P("band", ("dx", "dy")))
    return jax.shard_map(on_device, mesh=mesh, in_specs=in_specs, out_specs=out_specs, check_vma=False)
```

time: 60.6 us -> 54.6 us (0.901)
  local copies, waits for them, and re-layouts: 4.04 us -> 0 us
  Pallas kernels: 53.9 us -> 51.8 us
    unnamed x11 -> x0, local copies, waits for them, and re-layouts: 2.72 us -> none
    pallas_call x1 -> x2, Pallas kernels: 53.9 us -> 51.8 us  [the longest x1 49.6 us: on_device(): pl.pallas_call(kernel, out_shape=(block, jax.ShapeDtypeStruct((8, ATOMS),...]
    pallas_call x2 -> x0, local copies, waits for them, and re-layouts: 1.32 us -> none  [on_device(): pl.pallas_call(kernel, out_shape=(jax.ShapeDtypeStruct((ORB, VEC, ATOMS),...]
where the time goes in v2:
time: 54.6 us; the launch traced here: 53.7 us
  Pallas kernels  51.8 us (95%)
  between operations  1.93 us (4%)
    pallas_call x1, Pallas kernels, on_device(): pl.pallas_call(kernel, out_shape=(block, jax.ShapeDtypeStruct((8, ATOMS),...  49.6 us
    pallas_call x1, Pallas kernels, on_device(): pl.pallas_call(hand_over, out_shape=(block, small, small), in_specs=[vmem...  2.22 us

profile of v2, /device:TPU:6, one launch (start us, length us, event | category | flops | bytes accessed | tf_op | source)
XLA Modules:
  0.0 53.7 jit_solution(12767160576122518645)
XLA Ops:
  1.9 49.6 %chebyshev.1 = (bf16[13,64,128]{2,1,0:T(8,128)(2,1)}, f32[8,128]{1,0:T(8,128)}) custom-call(bf16[13,64,128]{2,1,0:T(8,128)(2,1)} %vec_in.1, s32[6,128]{1,0:T(8,128)} %pairs_in.1, s32[128]{0:T(128)} %count_in.1, bf16[6,13,13,128]{3,2,1,0:T(8,128)(2,1)} %blocks_in.1, bf16[13,13,4,16]{3,2,1,0:T(4,128)(2,1)} %bitcast.4, bf16[13,13,4,16]{3,2,1,0:T(4,128)(2,1)} %bitcast.5, ...), custom_call_target="tpu_custom_call" | custom-call | tf_op jit(solution)/shard_map/chebyshev/pallas_call | solution.py:414
  51.5 2.2 %hand_over.1 = (bf16[13,64,128]{2,1,0:T(8,128)(2,1)}, f32[8,64]{1,0:T(8,128)}, f32[8,64]{1,0:T(8,128)}) custom-call(bf16[13,64,128]{2,1,0:T(8,128)(2,1)} %get-tuple-element.8.filtered, f32[8,128]{1,0:T(8,128)} %get-tuple-element.9.sums), custom_call_target="tpu_custom_call" | custom-call | tf_op jit(solution)/shard_map/hand_over/pallas_call | solution.py:460

commit v3 on v2

--- a/solution.py
+++ b/solution.py
@@ -31,9 +31,9 @@
 
 
 def kernel(
-    vec_in, pairs_in, count_in, blocks_in, cx_in, cy_in, top_ref, cut_ref,
+    vec_in, pairs_in, count_in, blocks_in, cx_in, cy_in, top_in, cut_in,
     filt_out, sums_out,
-    field, pairs, count, blocks, cross, spread, chosen, double, lines, inner, whole, rim, rim_got, rim_lines, rim_sent, rim_came,
+    field, top_ref, cut_ref, pairs, count, blocks, cross, spread, chosen, double, lines, inner, whole, rim, rim_got, rim_lines, rim_sent, rim_came,
     strips, strips_got, total, inside, added, right_side, prev_got, next_got, far_got,
     ysend, ygot, zsend, zgot,
     load_sem, store_sem, rim_send, rim_recv, strip_send, strip_recv, ring_send, ring_recv,
@@ -59,6 +59,8 @@
                 (pairs_in, pairs),
                 (count_in, count),
                 (blocks_in, blocks),
+                (top_in, top_ref),
+                (cut_in, cut_ref),
             )
         )
     ]
@@ -231,7 +233,7 @@
             strip_copies(step + 1)[s].start()
 
     def finish(step, scale, keep):
-        for o in range(ORB):
+        for o in (0, 1, 2, 3, 7, 8, 9, 4, 5, 6, 10, 11, 12):
             tile = o // 8
             rows = jnp.zeros((VEC, ATOMS), F32)
             for s in range(4):
@@ -245,6 +247,9 @@
             if keep is not None:
                 result = result - field[keep, o].astype(F32)
             field[step + 1, o] = result.astype(BF16)
+            if step == 2:
+                for index in {3: (0,), 9: (1,), 6: (2, 5), 12: (3, 4)}.get(o, ()):
+                    ring_copies[index].start()
 
     own_rows = pl.ds(pl.multiple_of(core * 2 * VEC, 2 * VEC), VEC)
     own_image_rows = pl.ds(pl.multiple_of(core * 2 * VEC + VEC, VEC), VEC)
@@ -288,8 +293,6 @@
         keep = {1: 0, 2: 1}.get(step)
         factor = 1.0 if step in (0, 3) else 2.0
         if step == 3:
-            for copy in ring_copies:
-                copy.start()
             pair_copies[0].start()
             store.start()
         interior(step)
@@ -395,29 +398,48 @@
     store.wait()
 
 
-def hand_over(filtered, sums, filt_out, corr_out, proj_out, sem):
-    copy = pltpu.make_async_copy(filtered, filt_out, sem)
-    copy.start()
-    corr_out[...] = sums[:, 0:VEC]
-    proj_out[...] = sums[:, VEC:]
-    copy.wait()
+def hand_over(filtered, sums, filt_out, corr_out, proj_out, held, held_sums, corr, proj, load_sem, store_sem):
+    parts = [pl.ds(first, last - first) for first, last in ((0, 3), (3, 6), (6, 9), (9, ORB))]
+    loads = [
+        pltpu.make_async_copy(filtered.at[part], held.at[part], load_sem.at[index]) for index, part in enumerate(parts)
+    ]
+    stores = [
+        pltpu.make_async_copy(held.at[part], filt_out.at[part], store_sem.at[index]) for index, part in enumerate(parts)
+    ]
+    load_sums = pltpu.make_async_copy(sums, held_sums, load_sem.at[4])
+    load_sums.start()
+    for load in loads:
+        load.start()
+    stores.append(pltpu.make_async_copy(corr, corr_out, store_sem.at[4]))
+    stores.append(pltpu.make_async_copy(proj, proj_out, store_sem.at[5]))
+    load_sums.wait()
+    corr[...] = held_sums[:, 0:VEC]
+    proj[...] = held_sums[:, VEC:]
+    stores[4].start()
+    stores[5].start()
+    for load, store in zip(loads, stores):
+        load.wait()
+        store.start()
+    for store in stores:
+        store.wait()
 
 
 def on_device(vectors, inner_pairs, inner_count, inner_blocks, cross_x_blocks, cross_y_blocks, spectrum_top, filter_cut):
     any_spec = pl.BlockSpec(memory_space=pl.ANY)
     hbm_spec = pl.BlockSpec(memory_space=pltpu.HBM)
     vmem_spec = pl.BlockSpec(memory_space=pltpu.VMEM)
-    smem_spec = pl.BlockSpec(memory_space=pltpu.SMEM)
     dma = pltpu.SemaphoreType.DMA
     block = jax.ShapeDtypeStruct((ORB, VEC, ATOMS), BF16)
     small = jax.ShapeDtypeStruct((8, VEC), F32)
     filtered, sums = pl.pallas_call(
         kernel,
         out_shape=(block, jax.ShapeDtypeStruct((8, ATOMS), F32)),
-        in_specs=[hbm_spec] * 6 + [smem_spec] * 2,
+        in_specs=[hbm_spec] * 8,
         out_specs=(any_spec, vmem_spec),
         scratch_shapes=[
             pltpu.VMEM((5, ORB, VEC, ATOMS), BF16),
+            pltpu.SMEM((1,), F32),
+            pltpu.SMEM((1,), F32),
             pltpu.VMEM((SLOTS, ATOMS), jnp.int32),
             pltpu.VMEM((ATOMS,), jnp.int32),
             pltpu.VMEM((SLOTS, ORB, ORB, ATOMS), BF16),
@@ -446,7 +468,7 @@
             pltpu.VMEM((2 * NY, VEC, ATOMS), BF16),
             pltpu.VMEM((NZ, 8, ATOMS), F32),
             pltpu.VMEM((NZ, 8, ATOMS), F32),
-            dma((6,)), dma(()), dma((2,)), dma((2,)), dma((4, 4)), dma((4, 4)), dma((10,)), dma((10,)),
+            dma((8,)), dma(()), dma((2,)), dma((2,)), dma((4, 4)), dma((4, 4)), dma((10,)), dma((10,)),
             dma((2,)), dma((2,)), dma((2, 2 * NY)), dma((2, 2 * NY)), dma((NZ,)), dma((NZ,)),
         ],
         compiler_params=pltpu.CompilerParams(
@@ -460,9 +482,12 @@
     filtered, correlation, projected = pl.pallas_call(
         hand_over,
         out_shape=(block, small, small),
-        in_specs=[vmem_spec, vmem_spec],
-        out_specs=(any_spec, vmem_spec, vmem_spec),
-        scratch_shapes=[dma(())],
+        in_specs=[any_spec, any_spec],
+        out_specs=(any_spec, any_spec, any_spec),
+        scratch_shapes=[
+            pltpu.VMEM((ORB, VEC, ATOMS), BF16), pltpu.VMEM((8, ATOMS), F32), pltpu.VMEM((8, VEC), F32),
+            pltpu.VMEM((8, VEC), F32), dma((5,)), dma((6,)),
+        ],
         compiler_params=pltpu.CompilerParams(vmem_limit_bytes=VMEM_BYTES),
         name="hand_over",
     )(filtered, sums)

time: 54.6 us -> 54.1 us (level)
  Pallas kernels: 51.8 us -> 51.2 us
    pallas_call x1, Pallas kernels: 2.22 us -> 1.65 us  [on_device(): pl.pallas_call(hand_over, out_shape=(block, small, small), in_specs=[any_...]
where the time goes in v3:
time: 54.1 us; the launch traced here: 53.1 us
  Pallas kernels  51.2 us (95%)
  between operations  1.93 us (4%)
    pallas_call x1, Pallas kernels, on_device(): pl.pallas_call(kernel, out_shape=(block, jax.ShapeDtypeStruct((8, ATOMS),...  49.5 us
    pallas_call x1, Pallas kernels, on_device(): pl.pallas_call(hand_over, out_shape=(block, small, small), in_specs=[any_...  1.65 us

profile of v3, /device:TPU:6, one launch (start us, length us, event | category | flops | bytes accessed | tf_op | source)
XLA Modules:
  0.0 53.1 jit_solution(7940271087351342145)
XLA Ops:
  1.9 49.5 %chebyshev.1 = (bf16[13,64,128]{2,1,0:T(8,128)(2,1)}, f32[8,128]{1,0:T(8,128)}) custom-call(bf16[13,64,128]{2,1,0:T(8,128)(2,1)} %vec_in.1, s32[6,128]{1,0:T(8,128)} %pairs_in.1, s32[128]{0:T(128)} %count_in.1, bf16[6,13,13,128]{3,2,1,0:T(8,128)(2,1)} %blocks_in.1, bf16[13,13,4,16]{3,2,1,0:T(4,128)(2,1)} %bitcast.4, bf16[13,13,4,16]{3,2,1,0:T(4,128)(2,1)} %bitcast.5, ...), custom_call_target="tpu_custom_call" | custom-call | tf_op jit(solution)/shard_map/chebyshev/pallas_call | solution.py:434
  51.5 1.7 %hand_over.1 = (bf16[13,64,128]{2,1,0:T(8,128)(2,1)}, f32[8,64]{1,0:T(8,128)}, f32[8,64]{1,0:T(8,128)}) custom-call(bf16[13,64,128]{2,1,0:T(8,128)(2,1)} %get-tuple-element.8.filtered, f32[8,128]{1,0:T(8,128)} %get-tuple-element.9.sums), custom_call_target="tpu_custom_call" | custom-call | tf_op jit(solution)/shard_map/hand_over/pallas_call | solution.py:482

commit v4 on v3

--- a/solution.py
+++ b/solution.py
@@ -378,13 +378,6 @@
 
     lax.fori_loop(0, NZ - 1, z_start, 0)
 
-    def z_take(step, value):
-        z_copy(step).wait_recv()
-        return value + zgot[step]
-
-    final = lax.fori_loop(1, NZ, z_take, zsend[dx]) * (1.0 / (ORB * ATOMS * NZ * NY))
-    sums_out[...] = final
-
     def z_end(step, carry):
         z_copy(step).wait_send()
         return carry
@@ -396,6 +389,15 @@
     for copy in rim_copies + ring_copies + passed_on + pair_copies + y_copies:
         copy.wait_send()
     store.wait()
+
+    def z_take(index, value):
+        near = (index + 1) // 2
+        step = near + (1 - index % 2) * (NZ - 2 * near)
+        z_copy(step).wait_recv()
+        return value + zgot[step]
+
+    final = lax.fori_loop(1, NZ, z_take, zsend[dx]) * (1.0 / (ORB * ATOMS * NZ * NY))
+    sums_out[...] = final
 
 
 def hand_over(filtered, sums, filt_out, corr_out, proj_out, held, held_sums, corr, proj, load_sem, store_sem):

time: 54.1 us -> 53.9 us (level)
  no operation moved by 1% of the time
where the time goes in v4:
time: 53.9 us; the launch traced here: 52.9 us
  Pallas kernels  51 us (95%)
  between operations  1.93 us (4%)
    pallas_call x1, Pallas kernels, on_device(): pl.pallas_call(kernel, out_shape=(block, jax.ShapeDtypeStruct((8, ATOMS),...  49.3 us
    pallas_call x1, Pallas kernels, on_device(): pl.pallas_call(hand_over, out_shape=(block, small, small), in_specs=[any_...  1.65 us

profile of v4, /device:TPU:6, one launch (start us, length us, event | category | flops | bytes accessed | tf_op | source)
XLA Modules:
  0.0 52.9 jit_solution(2381370743446501411)
XLA Ops:
  1.9 49.3 %chebyshev.1 = (bf16[13,64,128]{2,1,0:T(8,128)(2,1)}, f32[8,128]{1,0:T(8,128)}) custom-call(bf16[13,64,128]{2,1,0:T(8,128)(2,1)} %vec_in.1, s32[6,128]{1,0:T(8,128)} %pairs_in.1, s32[128]{0:T(128)} %count_in.1, bf16[6,13,13,128]{3,2,1,0:T(8,128)(2,1)} %blocks_in.1, bf16[13,13,4,16]{3,2,1,0:T(4,128)(2,1)} %bitcast.4, bf16[13,13,4,16]{3,2,1,0:T(4,128)(2,1)} %bitcast.5, ...), custom_call_target="tpu_custom_call" | custom-call | tf_op jit(solution)/shard_map/chebyshev/pallas_call | solution.py:436
  51.3 1.7 %hand_over.1 = (bf16[13,64,128]{2,1,0:T(8,128)(2,1)}, f32[8,64]{1,0:T(8,128)}, f32[8,64]{1,0:T(8,128)}) custom-call(bf16[13,64,128]{2,1,0:T(8,128)(2,1)} %get-tuple-element.8.filtered, f32[8,128]{1,0:T(8,128)} %get-tuple-element.9.sums), custom_call_target="tpu_custom_call" | custom-call | tf_op jit(solution)/shard_map/hand_over/pallas_call | solution.py:484
